TPU v7x, 1024 devices: a whole 4x8x16 slice. The times are simulated.
1024 devices in a mesh: section: 16 (over z), expert: 64 (over x, y, core).
Axes of the slice: x: 4, y: 8, z: 16, core: 2. Of those that a mesh axis runs over, the one named last changes fastest.
Arguments:
- section_inputs: bfloat16 [16, 4096, 2560], P('section', 'expert'), may hold values from -6 to 6
- incoming: bfloat16 [1, 4096, 2560], P(None, 'expert'), may hold values from -6 to 6
- norm_gain: float32 [16, 2560], P('section'), may hold values from 0.5 to 1.5
- in_weights: bfloat16 [16, 40960, 1536], P('section', 'expert'), may hold values from -0.125 to 0.125
- down_weights: bfloat16 [16, 40960, 768], P('section', 'expert'), may hold values from -0.21875 to 0.21875
- expert_ids: int32 [2, 16, 4096, 2], P(None, 'section', 'expert'), may hold values from 0 to 15, all different within a row; in each aligned block of 64 rows (0 to 63, 64 to 127, ..., all dimensions but the last counted through in order) at most 10 rows name the same one
- route_weights: float32 [2, 16, 4096, 2], P(None, 'section', 'expert'), may hold values from 0.2 to 1
Outputs:
- final_state: bfloat16 [16, 4096, 2560], P('section', 'expert')
Inputs may be any that keep to these rules, and one draw needn't show every extreme that they name: `expert_ids`: in each aligned block of 64 tokens (the tokens of one index of expert) of one step and section, no expert is named by more than 10 tokens; a token names 2 different experts.
All inputs are finite; a program needn't handle non-finite values.
Results may differ from a plain program's by a relative error of at most 0.019.
Values may be sent and summed in bfloat16 or wider, within the bound.
A program may use at most 32 MiB of HBM per device.

v0:
```python
import jax
import jax.numpy as jnp
from jax import lax
from jax.sharding import PartitionSpec as P

GROUP = 4
TOPK = 2
TICKS = 2


def swapped(block, axis, apart):
    count = lax.axis_size(axis)
    route = []
    for low in range(count):
        high = low | 1 << apart
        if high != low and high < count:
            route += [(low, high), (high, low)]
    return lax.ppermute(block, axis, route)


def from_behind(block, axis, distance):
    devices = range(lax.axis_size(axis))
    route = [(i - distance, i) for i in devices if i - distance in devices]
    return lax.ppermute(block, axis, route)


def norm_rows(inputs, scale_row):
    widened = inputs.astype(jnp.float32)
    mean_square = jnp.mean(widened * widened, axis=-1, keepdims=True)
    return (widened * lax.rsqrt(mean_square + 1e-06) * scale_row).astype(jnp.bfloat16)


def slot_tables(block_ids, block_weights, expert_count, capacity, token_count):
    flat_ids = block_ids.reshape(-1)
    flat_weights = block_weights.reshape(-1)
    onehot = (flat_ids[:, None] == jnp.arange(expert_count, dtype=jnp.int32)[None, :]).astype(
        jnp.int32
    )
    before = jnp.cumsum(onehot, axis=0) - onehot
    slot_index = jnp.sum(before * onehot, axis=1)
    slot_hot = (slot_index[:, None] == jnp.arange(capacity, dtype=jnp.int32)[None, :]).astype(
        jnp.float32
    )
    token_of = jnp.arange(token_count * TOPK, dtype=jnp.int32) // TOPK
    owner = (token_of[:, None] == jnp.arange(token_count, dtype=jnp.int32)[None, :]).astype(
        jnp.float32
    )
    expert_hot = onehot.astype(jnp.float32)
    picker = jnp.einsum("ae,ac,at->ect", expert_hot, slot_hot, owner)
    blender = jnp.einsum("ae,ac,at,a->tec", expert_hot, slot_hot, owner, flat_weights)
    return (picker, blender)


def body(section_inputs, incoming, norm_gain, in_weights, down_weights, expert_ids, route_weights):
    axis_span = lax.axis_size("expert")
    group_size = GROUP
    expert_count = axis_span // group_size
    token_count = section_inputs.shape[1]
    capacity = min(token_count, max(2, TOPK * token_count * 5 // (4 * expert_count)))
    levels = group_size.bit_length() - 1
    position = lax.axis_index("expert")
    slice_width = in_weights.shape[1]
    hidden_units = down_weights.shape[2]
    bit_sequence = list(range(levels))
    carried = section_inputs[0]
    for step_index in range(TICKS):
        normed = norm_rows(carried, norm_gain[0])
        picker, blender = slot_tables(
            expert_ids[step_index, 0],
            route_weights[step_index, 0],
            expert_count,
            capacity,
            token_count,
        )
        outgoing = jnp.einsum(
            "ect,tgd->egcd",
            picker.astype(jnp.bfloat16),
            normed.reshape(token_count, group_size, slice_width),
            preferred_element_type=jnp.float32,
        ).astype(jnp.bfloat16)
        outgoing = outgoing.reshape(expert_count * group_size, capacity, slice_width)
        layer_received = lax.all_to_all(outgoing, "expert", split_axis=0, concat_axis=0, tiled=True)
        slot_count = layer_received.shape[1]
        row_total = axis_span * slot_count
        token_rows = layer_received.reshape(row_total, slice_width)
        partial_value = jnp.dot(
            token_rows, in_weights[0], preferred_element_type=jnp.float32
        ).astype(jnp.bfloat16)
        current = partial_value.reshape(row_total, 2, hidden_units).astype(jnp.float32)
        for bit_number in bit_sequence:
            bit_value = position >> bit_number & 1
            half_size = current.shape[2] // 2
            lower_half = current[:, :, :half_size]
            upper_half = current[:, :, half_size:]
            kept_half = jnp.where(bit_value == 1, upper_half, lower_half)
            sent_half = jnp.where(bit_value == 1, lower_half, upper_half).astype(jnp.bfloat16)
            arrived = swapped(sent_half, "expert", bit_number)
            current = kept_half + arrived.astype(jnp.float32)
        pieces = (jax.nn.silu(current[:, 0]) * current[:, 1]).astype(jnp.bfloat16)
        for bit_number in reversed(bit_sequence):
            bit_value = position >> bit_number & 1
            partner = swapped(pieces, "expert", bit_number)
            pieces = jnp.where(
                bit_value == 1,
                jnp.concatenate([partner, pieces], axis=1),
                jnp.concatenate([pieces, partner], axis=1),
            )
        produced = lax.dot_general(
            pieces, down_weights[0], (((1,), (1,)), ((), ())), preferred_element_type=jnp.float32
        ).astype(jnp.bfloat16)
        produced = produced.reshape(axis_span, slot_count, slice_width)
        returned = lax.all_to_all(produced, "expert", split_axis=0, concat_axis=0, tiled=True)
        returned = returned.reshape(expert_count, group_size, capacity, slice_width)
        mixture = jnp.einsum("tec,egcd->tgd", blender, returned.astype(jnp.float32))
        carried = (
            carried.astype(jnp.float32) + mixture.reshape(token_count, group_size * slice_width)
        ).astype(jnp.bfloat16)
        if step_index + 1 < TICKS:
            handed = from_behind(carried, "section", 1)
            is_first = lax.axis_index("section") == 0
            carried = jnp.where(is_first, incoming[step_index], handed)
    return carried[None]


def solution(mesh):
    placed = (
        P("section", "expert", None),
        P(None, "expert", None),
        P("section", None),
        P("section", "expert", None),
        P("section", "expert", None),
        P(None, "section", "expert", None),
        P(None, "section", "expert", None),
    )
    return jax.shard_map(
        body, mesh=mesh, in_specs=placed, out_specs=P("section", "expert", None), check_vma=False
    )
```

profile of v0, /device:TPU:1, one launch (start us, length us, event | category | flops | bytes accessed | tf_op | source)
XLA Modules:
  0.0 303.6 jit_solution(7451633180110721463)
XLA Ops:
  0.0 1.3 reshape.96
  1.3 1.1 fusion.30
  5.2 1.3 copy.65
  6.6 18.2 %all-to-all-start = ((bf16[64,10,640]{2,1,0:T(8,128)(2,1)}), bf16[64,10,640]{2,1,0:T(8,128)(2,1)S(1)}, u32[]{:S(2)}, u32[]{:S(2)}) async-start(bf16[64,10,640]{2,1,0:T(8,128)(2,1)} %bitcast.128), calls=%async_computation | async-start | bytes 2621440 | tf_op jit(solution)/shard_map/all_to_all | solution.py:82
  24.8 34.2 %all-to-all-done = bf16[64,10,640]{2,1,0:T(8,128)(2,1)S(1)} async-done(((bf16[64,10,640]{2,1,0:T(8,128)(2,1)}), bf16[64,10,640]{2,1,0:T(8,128)(2,1)S(1)}, u32[]{:S(2)}, u32[]{:S(2)}) %all-to-all-start) | async-done | bytes 819232 | tf_op jit(solution)/shard_map/all_to_all | solution.py:82
  59.0 1.1 reshape.87
  60.1 4.7 %fusion.6 = f32[640,1536]{1,0:T(8,128)} fusion(bf16[640,640]{1,0:T(8,128)(2,1)} %reshape.87, bf16[1,640,1536]{2,1,0:T(8,128)(2,1)S(1)} %copy-done), kind=kOutput, calls=%fused_computation.10 | convolution fusion | flops 1260257280 | bytes 6717440 | tf_op jit(solution)/shard_map/dot_general | solution.py:86
  64.8 5.4 %copy.70 = f32[640,1536]{0,1:T(8,128)} copy(f32[640,1536]{1,0:T(8,128)} %fusion.6) | data formatting | bytes 7864320 | tf_op jit(solution)/shard_map/convert_element_type | solution.py:89
  70.3 3.3 %select_convert_fusion.1 = bf16[640,2,384]{0,2,1:T(8,128)(2,1)} fusion(f32[640,2,768]{0,2,1:T(8,128)} %bitcast.122, pred[]{:T(512)S(6)} %eq.124), kind=kLoop, calls=%fused_computation.16 | loop fusion | flops 491520 | bytes 2949121 | tf_op jit(solution)/shard_map/convert_element_type | solution.py:96
  73.5 1.9 collective-permute-start
  75.5 2.7 collective-permute-done
  78.2 2.4 convert_add_fusion.1
  80.7 2.6 collective-permute-start.1
  83.3 12.0 %collective-permute-done.1 = bf16[640,2,192]{0,2,1:T(8,128)(2,1)S(1)} collective-permute-done((bf16[640,2,192]{0,2,1:T(8,128)(2,1)S(1)}, bf16[640,2,192]{0,2,1:T(8,128)(2,1)S(1)}, u32[]{:S(2)}, u32[]{:S(2)}) %collective-permute-start.1) | collective-permute-done | bytes 491552 | tf_op jit(solution)/shard_map/ppermute | solution.py:18
  95.6 2.5 collective-permute-start.2
  98.1 6.0 %collective-permute-done.2 = bf16[640,192]{0,1:T(8,128)(2,1)S(1)} collective-permute-done((bf16[640,192]{0,1:T(8,128)(2,1)S(1)}, bf16[640,192]{0,1:T(8,128)(2,1)S(1)}, u32[]{:S(2)}, u32[]{:S(2)}) %collective-permute-start.2) | collective-permute-done | bytes 245792 | tf_op jit(solution)/shard_map/ppermute | solution.py:18
  104.3 3.8 %collective-permute-start.3 = (bf16[640,384]{0,1:T(8,128)(2,1)S(1)}, bf16[640,384]{0,1:T(8,128)(2,1)S(1)}, u32[]{:S(2)}, u32[]{:S(2)}) collective-permute-start(bf16[640,384]{0,1:T(8,128)(2,1)S(1)} %maximum_select_fusion.4), channel_id=1, source_target_pairs={{0,1},{1,0},{2,3},{3,2},{4,5},{5,4},{6,7},{7,6},{8,9},{9,8},{10,11... | collective-permute-start | bytes 1474568 | tf_op jit(solution)/shard_map/ppermute | solution.py:18
  108.0 1.5 collective-permute-done.3
  109.5 1.0 convolution_convert_fusion.3
  110.6 1.2 reshape.88
  111.8 6.1 %all-to-all-start.1 = ((bf16[64,10,640]{2,1,0:T(8,128)(2,1)}), bf16[64,10,640]{2,1,0:T(8,128)(2,1)S(1)}, u32[]{:S(2)}, u32[]{:S(2)}) async-start(bf16[64,10,640]{2,1,0:T(8,128)(2,1)} %reshape.88), calls=%async_computation.1 | async-start | bytes 2621440 | tf_op jit(solution)/shard_map/all_to_all | solution.py:112
  119.3 32.8 %all-to-all-done.1 = bf16[64,10,640]{2,1,0:T(8,128)(2,1)S(1)} async-done(((bf16[64,10,640]{2,1,0:T(8,128)(2,1)}), bf16[64,10,640]{2,1,0:T(8,128)(2,1)S(1)}, u32[]{:S(2)}, u32[]{:S(2)}) %all-to-all-start.1) | async-done | bytes 819232 | tf_op jit(solution)/shard_map/all_to_all | solution.py:112
  152.1 1.2 copy.86
  153.3 1.7 dot_general.91
  155.0 1.4 fusion.2
  156.5 1.3 collective-permute-start.4
  158.0 7.2 %collective-permute-done.4 = bf16[64,2560]{1,0:T(8,128)(2,1)S(1)} collective-permute-done((bf16[64,2560]{1,0:T(8,128)(2,1)S(1)}, bf16[64,2560]{1,0:T(8,128)(2,1)S(1)}, u32[]{:S(2)}, u32[]{:S(2)}) %collective-permute-start.4) | collective-permute-done | bytes 327712 | tf_op jit(solution)/shard_map/ppermute | solution.py:24
  167.1 39.5 %all_to_all.20 = bf16[64,10,640]{2,1,0:T(8,128)(2,1)S(1)} all-to-all(bf16[64,10,640]{2,1,0:T(8,128)(2,1)S(1)} %bitcast.129), channel_id=1, replica_groups=mesh['section'=16,'expert'=64] {'expert'}, dimensions={0} | all-to-all | bytes 1638400 | tf_op jit(solution)/shard_map/all_to_all | solution.py:82
  206.6 1.1 reshape.92
  207.7 4.7 %fusion.5 = f32[640,1536]{1,0:T(8,128)} fusion(bf16[640,640]{1,0:T(8,128)(2,1)} %reshape.92, bf16[1,640,1536]{2,1,0:T(8,128)(2,1)S(1)} %copy-done), kind=kOutput, calls=%fused_computation.8 | convolution fusion | flops 1260257280 | bytes 6717440 | tf_op jit(solution)/shard_map/dot_general | solution.py:86
  212.4 5.4 %copy.72 = f32[640,1536]{0,1:T(8,128)} copy(f32[640,1536]{1,0:T(8,128)} %fusion.5) | data formatting | bytes 7864320 | tf_op jit(solution)/shard_map/convert_element_type | solution.py:89
  217.9 2.3 select_convert_fusion
  220.2 1.9 collective-permute-start.5
  222.1 2.5 collective-permute-done.5
  224.7 2.5 convert_add_fusion
  227.2 2.5 collective-permute-start.6
  229.8 12.1 %collective-permute-done.6 = bf16[640,2,192]{0,2,1:T(8,128)(2,1)S(1)} collective-permute-done((bf16[640,2,192]{0,2,1:T(8,128)(2,1)S(1)}, bf16[640,2,192]{0,2,1:T(8,128)(2,1)S(1)}, u32[]{:S(2)}, u32[]{:S(2)}) %collective-permute-start.6) | collective-permute-done | bytes 491552 | tf_op jit(solution)/shard_map/ppermute | solution.py:18
  242.1 2.4 collective-permute-start.7
  244.5 6.1 %collective-permute-done.7 = bf16[640,192]{0,1:T(8,128)(2,1)S(1)} collective-permute-done((bf16[640,192]{0,1:T(8,128)(2,1)S(1)}, bf16[640,192]{0,1:T(8,128)(2,1)S(1)}, u32[]{:S(2)}, u32[]{:S(2)}) %collective-permute-start.7) | collective-permute-done | bytes 245792 | tf_op jit(solution)/shard_map/ppermute | solution.py:18
  250.8 3.8 %collective-permute-start.8 = (bf16[640,384]{0,1:T(8,128)(2,1)S(1)}, bf16[640,384]{0,1:T(8,128)(2,1)S(1)}, u32[]{:S(2)}, u32[]{:S(2)}) collective-permute-start(bf16[640,384]{0,1:T(8,128)(2,1)S(1)} %maximum_select_fusion.5), channel_id=1, source_target_pairs={{0,1},{1,0},{2,3},{3,2},{4,5},{5,4},{6,7},{7,6},{8,9},{9,8},{10,11... | collective-permute-start | bytes 1474568 | tf_op jit(solution)/shard_map/ppermute | solution.py:18
  254.6 1.5 collective-permute-done.8
  256.1 1.0 convolution_convert_fusion.2
  257.1 1.2 reshape.93
  258.3 6.0 %all-to-all-start.3 = ((bf16[64,10,640]{2,1,0:T(8,128)(2,1)}), bf16[64,10,640]{2,1,0:T(8,128)(2,1)S(1)}, u32[]{:S(2)}, u32[]{:S(2)}) async-start(bf16[64,10,640]{2,1,0:T(8,128)(2,1)} %reshape.93), calls=%async_computation.3 | async-start | bytes 2621440 | tf_op jit(solution)/shard_map/all_to_all | solution.py:112
  264.6 33.9 %all-to-all-done.3 = bf16[64,10,640]{2,1,0:T(8,128)(2,1)S(1)} async-done(((bf16[64,10,640]{2,1,0:T(8,128)(2,1)}), bf16[64,10,640]{2,1,0:T(8,128)(2,1)S(1)}, u32[]{:S(2)}, u32[]{:S(2)}) %all-to-all-start.3) | async-done | bytes 819232 | tf_op jit(solution)/shard_map/all_to_all | solution.py:112
  298.5 1.2 copy.85
  299.7 1.7 dot_general.106
  301.4 2.2 fusion.4
  (55 shorter events, 7.5 us)
Async XLA Ops:
  0.0 60.1 %copy-start = (bf16[1,640,1536]{2,1,0:T(8,128)(2,1)S(1)}, bf16[1,640,1536]{2,1,0:T(8,128)(2,1)}, u32[]{:S(2)}) copy-start(bf16[1,640,1536]{2,1,0:T(8,128)(2,1)} %param.10) | copy-start | bytes 5898244
  6.6 52.5 %all-to-all-start = ((bf16[64,10,640]{2,1,0:T(8,128)(2,1)}), bf16[64,10,640]{2,1,0:T(8,128)(2,1)S(1)}, u32[]{:S(2)}, u32[]{:S(2)}) async-start(bf16[64,10,640]{2,1,0:T(8,128)(2,1)} %bitcast.128), calls=%async_computation | async-start | bytes 2621440 | tf_op jit(solution)/shard_map/all_to_all | solution.py:82
  73.5 4.7 %collective-permute-start = (bf16[640,2,384]{0,2,1:T(8,128)(2,1)}, bf16[640,2,384]{0,2,1:T(8,128)(2,1)S(1)}, u32[]{:S(2)}, u32[]{:S(2)}) collective-permute-start(bf16[640,2,384]{0,2,1:T(8,128)(2,1)} %select_convert_fusion.1), channel_id=1, source_target_pairs={{0,1},{1,0},{2,3},{3,2},{4,5},{5,4},{6,7},{7,6},{8,9},{9,8},{10,11... | collective-permute-start | bytes 2949128 | tf_op jit(solution)/shard_map/ppermute | solution.py:18
  80.7 14.6 %collective-permute-start.1 = (bf16[640,2,192]{0,2,1:T(8,128)(2,1)S(1)}, bf16[640,2,192]{0,2,1:T(8,128)(2,1)S(1)}, u32[]{:S(2)}, u32[]{:S(2)}) collective-permute-start(bf16[640,2,192]{0,2,1:T(8,128)(2,1)S(1)} %select_convert_fusion.3), channel_id=1, source_target_pairs={{0,2},{2,0},{1,3},{3,1},{4,6},{6,4},{5,7},{7,5},{8,10},{10,8},{9,1... | collective-permute-start | bytes 1474568 | tf_op jit(solution)/shard_map/ppermute | solution.py:18
  95.4 14.1 %copy-start.5 = (bf16[1,640,768]{2,1,0:T(8,128)(2,1)S(1)}, bf16[1,640,768]{2,1,0:T(8,128)(2,1)}, u32[]{:S(2)}) copy-start(bf16[1,640,768]{2,1,0:T(8,128)(2,1)} %param.11) | copy-start | bytes 2949124
  95.6 8.5 %collective-permute-start.2 = (bf16[640,192]{0,1:T(8,128)(2,1)S(1)}, bf16[640,192]{0,1:T(8,128)(2,1)S(1)}, u32[]{:S(2)}, u32[]{:S(2)}) collective-permute-start(bf16[640,192]{0,1:T(8,128)(2,1)S(1)} %fusion.36), channel_id=1, source_target_pairs={{0,2},{2,0},{1,3},{3,1},{4,6},{6,4},{5,7},{7,5},{8,10},{10,8},{9,1... | collective-permute-start | bytes 737288 | tf_op jit(solution)/shard_map/ppermute | solution.py:18
  104.3 5.2 %collective-permute-start.3 = (bf16[640,384]{0,1:T(8,128)(2,1)S(1)}, bf16[640,384]{0,1:T(8,128)(2,1)S(1)}, u32[]{:S(2)}, u32[]{:S(2)}) collective-permute-start(bf16[640,384]{0,1:T(8,128)(2,1)S(1)} %maximum_select_fusion.4), channel_id=1, source_target_pairs={{0,1},{1,0},{2,3},{3,2},{4,5},{5,4},{6,7},{7,6},{8,9},{9,8},{10,11... | collective-permute-start | bytes 1474568 | tf_op jit(solution)/shard_map/ppermute | solution.py:18
  110.5 7.3 %copy-start.4 = (f32[2,1,64,2]{2,3,1,0:T(2,128)S(1)}, f32[2,1,64,2]{2,3,1,0:T(2,128)}, u32[]{:S(2)}) copy-start(f32[2,1,64,2]{2,3,1,0:T(2,128)} %param.13) | copy-start | bytes 3076
  111.8 40.3 %all-to-all-start.1 = ((bf16[64,10,640]{2,1,0:T(8,128)(2,1)}), bf16[64,10,640]{2,1,0:T(8,128)(2,1)S(1)}, u32[]{:S(2)}, u32[]{:S(2)}) async-start(bf16[64,10,640]{2,1,0:T(8,128)(2,1)} %reshape.88), calls=%async_computation.1 | async-start | bytes 2621440 | tf_op jit(solution)/shard_map/all_to_all | solution.py:112
  153.3 11.9 %copy-start.2 = (bf16[1,64,2560]{2,1,0:T(8,128)(2,1)S(1)}, bf16[1,64,2560]{2,1,0:T(8,128)(2,1)}, u32[]{:S(2)}) copy-start(bf16[1,64,2560]{2,1,0:T(8,128)(2,1)} %param.8) | copy-start | bytes 983044
  156.5 8.7 %collective-permute-start.4 = (bf16[64,2560]{1,0:T(8,128)(2,1)S(1)}, bf16[64,2560]{1,0:T(8,128)(2,1)S(1)}, u32[]{:S(2)}, u32[]{:S(2)}) collective-permute-start(bf16[64,2560]{1,0:T(8,128)(2,1)S(1)} %fusion.2), channel_id=1, source_target_pairs={{0,64},{64,128},{128,192},{192,256},{256,320},{320,384},{384,448},... | collective-permute-start | bytes 983048 | tf_op jit(solution)/shard_map/ppermute | solution.py:24
  165.4 0.7 copy-start.1
  220.2 4.5 %collective-permute-start.5 = (bf16[640,2,384]{0,2,1:T(8,128)(2,1)S(1)}, bf16[640,2,384]{0,2,1:T(8,128)(2,1)S(1)}, u32[]{:S(2)}, u32[]{:S(2)}) collective-permute-start(bf16[640,2,384]{0,2,1:T(8,128)(2,1)S(1)} %select_convert_fusion), channel_id=1, source_target_pairs={{0,1},{1,0},{2,3},{3,2},{4,5},{5,4},{6,7},{7,6},{8,9},{9,8},{10,11... | collective-permute-start | bytes 2949128 | tf_op jit(solution)/shard_map/ppermute | solution.py:18
  227.2 14.6 %collective-permute-start.6 = (bf16[640,2,192]{0,2,1:T(8,128)(2,1)S(1)}, bf16[640,2,192]{0,2,1:T(8,128)(2,1)S(1)}, u32[]{:S(2)}, u32[]{:S(2)}) collective-permute-start(bf16[640,2,192]{0,2,1:T(8,128)(2,1)S(1)} %select_convert_fusion.2), channel_id=1, source_target_pairs={{0,2},{2,0},{1,3},{3,1},{4,6},{6,4},{5,7},{7,5},{8,10},{10,8},{9,1... | collective-permute-start | bytes 1474568 | tf_op jit(solution)/shard_map/ppermute | solution.py:18
  242.0 14.1 %copy-start.6 = (bf16[1,640,768]{2,1,0:T(8,128)(2,1)S(1)}, bf16[1,640,768]{2,1,0:T(8,128)(2,1)}, u32[]{:S(2)}) copy-start(bf16[1,640,768]{2,1,0:T(8,128)(2,1)} %param.11) | copy-start | bytes 2949124
  242.1 8.5 %collective-permute-start.7 = (bf16[640,192]{0,1:T(8,128)(2,1)S(1)}, bf16[640,192]{0,1:T(8,128)(2,1)S(1)}, u32[]{:S(2)}, u32[]{:S(2)}) collective-permute-start(bf16[640,192]{0,1:T(8,128)(2,1)S(1)} %fusion.34), channel_id=1, source_target_pairs={{0,2},{2,0},{1,3},{3,1},{4,6},{6,4},{5,7},{7,5},{8,10},{10,8},{9,1... | collective-permute-start | bytes 737288 | tf_op jit(solution)/shard_map/ppermute | solution.py:18
  250.8 5.2 %collective-permute-start.8 = (bf16[640,384]{0,1:T(8,128)(2,1)S(1)}, bf16[640,384]{0,1:T(8,128)(2,1)S(1)}, u32[]{:S(2)}, u32[]{:S(2)}) collective-permute-start(bf16[640,384]{0,1:T(8,128)(2,1)S(1)} %maximum_select_fusion.5), channel_id=1, source_target_pairs={{0,1},{1,0},{2,3},{3,2},{4,5},{5,4},{6,7},{7,6},{8,9},{9,8},{10,11... | collective-permute-start | bytes 1474568 | tf_op jit(solution)/shard_map/ppermute | solution.py:18
  257.1 7.3 %copy-start.3 = (f32[1,1,64,2]{2,3,1,0:T(2,128)S(1)}, f32[1,1,64,2]{2,3,1,0:T(2,128)}, u32[]{:S(2)}) copy-start(f32[1,1,64,2]{2,3,1,0:T(2,128)} %get-tuple-element.7) | copy-start | bytes 1540
  258.3 40.2 %all-to-all-start.3 = ((bf16[64,10,640]{2,1,0:T(8,128)(2,1)}), bf16[64,10,640]{2,1,0:T(8,128)(2,1)S(1)}, u32[]{:S(2)}, u32[]{:S(2)}) async-start(bf16[64,10,640]{2,1,0:T(8,128)(2,1)} %reshape.93), calls=%async_computation.3 | async-start | bytes 2621440 | tf_op jit(solution)/shard_map/all_to_all | solution.py:112
where the time goes:
time: 305 us; the launch traced here: 304 us
  waiting for transfers between devices  152 us (50%)
  starting transfers between devices  53 us (17%)
  blocking collectives  39.5 us (13%)
  local copies, waits for them, and re-layouts  27.4 us (9%)
  matrix products  16.1 us (5%)
  other arithmetic  14.7 us (5%)
    all_to_all x2, waiting for transfers between devices, body(): lax.all_to_all(produced, 'expert', split_axis=0, concat_axis=0, tiled=True)  66.7 us
    ppermute x8, waiting for transfers between devices, swapped(): return lax.ppermute(block, axis, route)  44.4 us
    all_to_all x1, blocking collectives, body(): lax.all_to_all(outgoing, 'expert', split_axis=0, concat_axis=0, tiled=True)  39.5 us
    all_to_all x1, waiting for transfers between devices, body(): lax.all_to_all(outgoing, 'expert', split_axis=0, concat_axis=0, tiled=True)  34.2 us
    ppermute x8, starting transfers between devices, swapped(): return lax.ppermute(block, axis, route)  21.4 us
    all_to_all x1, starting transfers between devices, body(): lax.all_to_all(outgoing, 'expert', split_axis=0, concat_axis=0, tiled=True)  18.2 us
    all_to_all x2, starting transfers between devices, body(): lax.all_to_all(produced, 'expert', split_axis=0, concat_axis=0, tiled=True)  12.1 us
    convert_element_type x2, local copies, waits for them, and re-layouts, body(): partial_value.reshape(row_total, 2, hidden_units).astype(jnp.float32)  10.9 us
  transfers between devices with their start and end apart: 12, of which 12 were waited for; matrix products, arithmetic and copies ran while one was open for 1% of the time, Pallas kernels for 0%

commit v1 on v0

v1 whole, which is shorter than its diff:
```python
import functools

import jax
import jax.numpy as jnp
from jax import lax
from jax.experimental import pallas as pl
from jax.experimental.pallas import tpu as pltpu
from jax.sharding import PartitionSpec as P

TICKS = 2
CAP = 10
NX = 4
MAIN = 16
REST = 4
BF16 = jnp.bfloat16
F32 = jnp.float32


def dot(a, b):
    return jnp.dot(a, b, preferred_element_type=F32)


def iota(shape, dim):
    return lax.broadcasted_iota(jnp.int32, shape, dim)


def slot_of(j, nx, ny):
    half = ny // 2
    experts = nx * half
    k = j - experts * MAIN
    rest_expert = ((k % (nx * REST)) // REST) * half + k // (nx * REST)
    is_main = j < experts * MAIN
    return jnp.where(is_main, j // MAIN, rest_expert), jnp.where(is_main, j % MAIN, MAIN + k % REST)


def kernel(
    dims,
    x_ref, inc_ref, gain_ref, win_hbm, wdn_hbm, ids_ref, rw_ref,
    out_ref,
    win, wdn, xs, wmeta, pm, bm, stat_s, stat_r, smain, srest, recv, yrest, xrest,
    part, core_in, kept, ysend, y_in, act, prod, back_x, back_y, ret, new, hand, fin,
    w_sem, swap_ss, swap_rs, meta_ss, meta_rs, stat_ss, stat_rs, main_ss, chunk_rs,
    yrest_ss, yrest_rs, xrest_ss, core_ss, core_rs, y_ss, y_rs, acty_ss, acty_rs,
    actc_ss, actc_rs, actf_ss, back_ss, backx_ss, backx_rs, backy_ss, back_rs,
    hand_ss, hand_rs, fin_ss, fin_rs,
):
    ns, nx, ny, tok, ds, ff, order, rest_at, fwd_slot = dims
    half = ny // 2
    experts = nx * half
    both = 2 * tok
    n_main = experts * MAIN
    n_rows = n_main + experts * REST
    n_chunk = half + 1
    main_rows = 2 * nx * MAIN
    rest_rows = nx * ny * REST
    yblk = nx * REST
    xblk = ny * REST
    width = 4 * ds

    s = lax.axis_index("section")
    me = lax.axis_index("expert")
    x = me // (2 * ny)
    y = (me // 2) % ny
    c = me % 2
    p = y % 2
    k = y // 2
    e = x * half + k

    def at(dx, to_y):
        return {"section": s, "expert": (((x + dx + nx) % nx) * ny + to_y) * 2 + c}

    far_x = sorted(range(nx), key=lambda dx: (-min(dx, nx - dx), dx))

    sibling = {"section": s, "expert": me + 1 - 2 * c}
    partner = {"section": s, "expert": (x * ny + y + 1 - 2 * p) * 2 + c}
    ahead = {"section": (s + 1) % ns, "expert": me}
    behind = {"section": (s + ns - 1) % ns, "expert": me}

    def send(src, dst, ss, rs, device):
        pltpu.make_async_remote_copy(
            src_ref=src, dst_ref=dst, send_sem=ss, recv_sem=rs, device_id=device,
            device_id_type=pl.DeviceIdType.MESH,
        ).start()

    def wait(ref, sem):
        pltpu.make_async_copy(ref, ref, sem).wait()

    def rows(start, count):
        return pl.ds(pl.multiple_of(start, count & -count), count)

    def columns(q, core):
        return pl.ds(pl.multiple_of(q * 2 * ds + core * ds, ds), ds)

    w_in = pltpu.make_async_copy(win_hbm.at[0], win, w_sem.at[0])
    w_down = pltpu.make_async_copy(wdn_hbm.at[0], wdn, w_sem.at[1])
    w_in.start()
    w_down.start()

    barrier = pltpu.get_barrier_semaphore()
    peers = [at(dx, (y + dy) % ny) for dy in range(ny) for dx in range(nx) if (dx, dy) != (0, 0)]
    peers += [sibling, ahead, behind]
    for device in peers:
        pl.semaphore_signal(barrier, inc=1, device_id=device, device_id_type=pl.DeviceIdType.MESH)

    own = rows(c * tok, tok)
    other = rows((1 - c) * tok, tok)
    lane = iota((tok, 128), 1)
    for t in range(TICKS):
        ids = ids_ref[t, 0]
        rw = rw_ref[t, 0]
        wmeta[t, own, :] = jnp.where(ids[:, 0:1] == lane, rw[:, 0:1], 0.0) + jnp.where(
            ids[:, 1:2] == lane, rw[:, 1:2], 0.0
        )
    for q in range(2):
        xs[0, q, own, :] = x_ref[0, :, columns(q, c)]
        xs[1, q, own, :] = inc_ref[0, :, columns(q, c)]
    pl.semaphore_wait(barrier, len(peers))

    for q in range(2):
        send(x_ref.at[0, :, columns(q, 1 - c)], xs.at[0, q, own, :], swap_ss.at[0, q], swap_rs.at[0, q], sibling)
    send(wmeta.at[:, own, :], wmeta.at[:, own, :], meta_ss, meta_rs, sibling)
    for q in range(2):
        send(inc_ref.at[0, :, columns(q, 1 - c)], xs.at[1, q, own, :], swap_ss.at[1, q], swap_rs.at[1, q], sibling)

    def earlier(shape, rank_dim):
        a, b = iota(shape, rank_dim), iota(shape, 1 - rank_dim)
        return ((b < a) & (b // tok == a // tok)).astype(BF16)

    def pick_table(t):
        w = jnp.transpose(wmeta[t])
        member = (w > 0).astype(BF16)
        number = dot(member, earlier((both, both), 1)) + (CAP * (iota((128, both), 1) // tok)).astype(F32)
        to_expert, to_number = slot_of(iota((n_rows, 128), 0), nx, ny)
        spread = (to_expert == iota((n_rows, 128), 1)).astype(BF16)
        _, to_number = slot_of(iota((n_rows, both), 0), nx, ny)
        hit = (dot(spread, member) > 0.5) & (dot(spread, number.astype(BF16)) == to_number.astype(F32))
        pm[t] = hit.astype(F32).astype(BF16)

    def blend_table(t):
        w = wmeta[t]
        member = (w > 0).astype(BF16)
        number = dot(earlier((both, both), 0), member) + (CAP * (iota((both, 128), 0) // tok)).astype(F32)
        to_expert, _ = slot_of(iota((128, n_rows), 1), nx, ny)
        spread = (to_expert == iota((128, n_rows), 0)).astype(BF16)
        _, to_number = slot_of(iota((both, n_rows), 1), nx, ny)
        hit = (dot(member, spread) > 0.5) & (dot(number.astype(BF16), spread) == to_number.astype(F32))
        bm[t] = jnp.where(hit, dot(w.astype(BF16), spread), 0.0).astype(BF16)

    def shuffle(out_dim):
        o = iota((rest_rows, rest_rows), out_dim)
        r = iota((rest_rows, rest_rows), 1 - out_dim)
        dx, source, j = o // xblk, (o % xblk) // REST, o % REST
        return (r == source * yblk + ((x - dx + nx) % nx) * REST + j).astype(F32).astype(BF16)

    def size(i):
        return rest_rows if i == rest_at else main_rows

    def pair_of(i):
        return order[i if i < rest_at else i - 1]

    parities = (p, 1 - p)

    def tick(t, carry):
        @pl.when(t == 0)
        def _():
            for q in range(2):
                wait(xs.at[0, q, other, :], swap_rs.at[0, q])

        square = jnp.zeros((both, 1), F32)
        for q in range(2):
            v = xs[t, q].astype(F32)
            square = square + jnp.sum(v * v, axis=-1, keepdims=True)
        stat_s[t] = jnp.broadcast_to(square, (both, 128))
        send(stat_s.at[t], stat_r.at[t], stat_ss.at[t], stat_rs.at[t], sibling)

        @pl.when(t == 0)
        def _():
            wait(wmeta.at[:, other, :], meta_rs)
            pick_table(0)

        wait(stat_r.at[t], stat_rs.at[t])
        scale = lax.rsqrt((square + stat_r[t, :, 0:1]) * (1.0 / width) + 1e-6)
        for q in range(2):
            normed = (xs[t, q].astype(F32) * scale * gain_ref[:, columns(q, c)]).astype(BF16)
            picked = dot(pm[t], normed).astype(BF16)
            smain[t, q * n_main : (q + 1) * n_main, :] = picked[:n_main]
            srest[t, q * half * yblk : (q + 1) * half * yblk, :] = picked[n_main:]

        for pairs in order:
            to_k = (k - pairs + half) % half
            dst = yrest.at[t, rows((2 * pairs + p) * yblk, yblk), :]
            for flip, to_p in enumerate(parities):
                src = srest.at[t, rows((to_p * half + to_k) * yblk, yblk), :]
                if pairs == 0 and flip == 0:
                    pltpu.make_async_copy(src, dst, yrest_rs.at[t]).start()
                else:
                    send(src, dst, yrest_ss.at[t], yrest_rs.at[t], at(0, 2 * to_k + to_p))
        for i in range(n_chunk):
            if i == rest_at:
                continue
            pairs = pair_of(i)
            to_k = (k - pairs + half) % half
            for flip, to_p in enumerate(parities):
                for dx in far_x:
                    to_x = (x - dx + nx) % nx
                    src = smain.at[t, rows(to_p * n_main + (to_x * half + to_k) * MAIN, MAIN), :]
                    dst = recv.at[t, i, rows((p * nx + dx) * MAIN, MAIN), :]
                    if pairs == 0 and flip == 0 and dx == 0:
                        pltpu.make_async_copy(src, dst, chunk_rs.at[t, i]).start()
                    else:
                        send(src, dst, main_ss.at[t], chunk_rs.at[t, i], at(-dx, 2 * to_k + to_p))

        @pl.when(t == 0)
        def _():
            blend_table(0)
            pick_table(1)
            blend_table(1)
            w_in.wait()
            w_down.wait()
            for q in range(2):
                wait(xs.at[1, q, other, :], swap_rs.at[1, q])

        def forward_rest():
            wait(yrest.at[t], yrest_rs.at[t])
            xrest[t] = dot(shuffle(0), yrest[t]).astype(BF16)
            for dx in range(nx):
                src = xrest.at[t, dx * xblk : (dx + 1) * xblk, :]
                dst = recv.at[t, rest_at, dx * xblk : (dx + 1) * xblk, :]
                if dx == 0:
                    pltpu.make_async_copy(src, dst, chunk_rs.at[t, rest_at]).start()
                else:
                    send(src, dst, xrest_ss.at[t], chunk_rs.at[t, rest_at], at(-dx, y))

        def stage_a(i):
            n = size(i)
            wait(recv.at[t, i, 0:n, :], chunk_rs.at[t, i])
            lhs = recv[t, i, 0:n, :]
            tile = ff // 2 if (ff // 2) % 128 == 0 else ff
            for j in range(0, 2 * ff, tile):
                part[t, i, 0:n, j : j + tile] = dot(lhs, win[:, j : j + tile]).astype(BF16)
            send(
                part.at[t, i, rows((1 - c) * (n // 2), n // 2), :], core_in.at[t, i, 0 : n // 2, :],
                core_ss.at[t, i], core_rs.at[t, i], sibling,
            )

        def stage_b(i):
            n = size(i)
            quarter = n // 4
            wait(core_in.at[t, i, 0 : n // 2, :], core_rs.at[t, i])

            def total(which):
                mine = part[t, i, rows(c * (n // 2) + which * quarter, quarter), :].astype(F32)
                return mine + core_in[t, i, rows(which * quarter, quarter), :].astype(F32)

            ysend[t, i, 0:quarter, :] = total(1 - p).astype(BF16)
            send(ysend.at[t, i, 0:quarter, :], y_in.at[t, i, 0:quarter, :], y_ss.at[t, i], y_rs.at[t, i], partner)
            kept[i, 0:quarter, :] = total(p)

        def stage_c(i):
            n = size(i)
            quarter = n // 4
            wait(y_in.at[t, i, 0:quarter, :], y_rs.at[t, i])
            pre = kept[i, 0:quarter, :] + y_in[t, i, 0:quarter, :].astype(F32)
            gate, up = pre[:, :ff], pre[:, ff:]
            mine = rows(c * (n // 2) + p * quarter, quarter)
            act[t, i, mine, :] = (gate / (1.0 + jnp.exp(-gate)) * up).astype(BF16)
            block = act.at[t, i, mine, :]
            send(block, block, acty_ss.at[t, i], acty_rs.at[t, i], partner)
            send(block, block, actc_ss.at[t, i], actc_rs.at[t, i], sibling)

        def stage_d(i):
            n = size(i)
            quarter = n // 4
            block = act.at[t, i, rows(c * (n // 2) + (1 - p) * quarter, quarter), :]
            wait(block, acty_rs.at[t, i])
            send(block, block, actf_ss.at[t, i], actc_rs.at[t, i], sibling)

        def stage_e(i):
            n = size(i)
            wait(act.at[t, i, rows((1 - c) * (n // 2), n // 2), :], actc_rs.at[t, i])
            prod[t, i, 0:n, :] = lax.dot_general(
                act[t, i, 0:n, :], wdn[...], (((1,), (1,)), ((), ())), preferred_element_type=F32
            ).astype(BF16)
            if i == rest_at:
                for dx in range(nx):
                    src = prod.at[t, i, dx * xblk : (dx + 1) * xblk, :]
                    dst = back_x.at[t, dx * xblk : (dx + 1) * xblk, :]
                    if dx == 0:
                        pltpu.make_async_copy(src, dst, backx_rs.at[t]).start()
                    else:
                        send(src, dst, backx_ss.at[t], backx_rs.at[t], at(dx, y))
                return
            dst = ret.at[t, p, rows(e * MAIN, MAIN), :]
            pairs = pair_of(i)
            to_k = (k + pairs) % half
            for flip, to_p in enumerate(parities):
                for dx in far_x:
                    src = prod.at[t, i, rows((to_p * nx + dx) * MAIN, MAIN), :]
                    if pairs == 0 and flip == 0 and dx == 0:
                        pltpu.make_async_copy(src, dst, back_rs.at[t]).start()
                    else:
                        send(src, dst, back_ss.at[t], back_rs.at[t], at(dx, 2 * to_k + to_p))

        def return_rest():
            wait(back_x.at[t], backx_rs.at[t])
            back_y[t] = dot(shuffle(1), back_x[t]).astype(BF16)
            dst = ret.at[t, p, rows(n_main + k * yblk, yblk), :]
            for pairs in order:
                to_k = (k + pairs) % half
                for flip, to_p in enumerate(parities):
                    src = back_y.at[t, rows((2 * pairs + to_p) * yblk, yblk), :]
                    if pairs == 0 and flip == 0:
                        pltpu.make_async_copy(src, dst, back_rs.at[t]).start()
                    else:
                        send(src, dst, backy_ss.at[t], back_rs.at[t], at(0, 2 * to_k + to_p))

        for n in range(n_chunk + 5):
            if n == rest_at + 5:
                return_rest()
            for lag, stage in ((4, stage_e), (3, stage_d), (2, stage_c), (1, stage_b)):
                if 0 <= n - lag < n_chunk:
                    stage(n - lag)
            if n == fwd_slot:
                forward_rest()
            if n < n_chunk:
                stage_a(n)

        wait(ret.at[t], back_rs.at[t])
        for q in range(2):
            mixed = dot(bm[t], ret[t, q])
            new[t, q] = (xs[t, q].astype(F32) + mixed).astype(BF16)

            @pl.when(t == 0)
            def _():
                send(new.at[0, q], hand.at[q], hand_ss.at[q], hand_rs.at[q], ahead)

            @pl.when(t == 1)
            def _():
                send(new.at[1, q, other, :], fin.at[q], fin_ss.at[q], fin_rs.at[q], sibling)

        @pl.when(t == 0)
        def _():
            for q in range(2):
                wait(hand.at[q], hand_rs.at[q])
                xs[1, q] = jnp.where(s == 0, xs[1, q], hand[q])

        return carry

    lax.fori_loop(0, TICKS, tick, 0)

    for q in range(2):
        out_ref[0, :, columns(q, c)] = new[1, q, own, :]
    for q in range(2):
        wait(fin.at[q], fin_rs.at[q])
        out_ref[0, :, columns(q, 1 - c)] = fin[q]

    for q in range(2):
        wait(xs.at[0, q, own, :], swap_ss.at[0, q])
        wait(xs.at[1, q, own, :], swap_ss.at[1, q])
        wait(hand.at[q], hand_ss.at[q])
        wait(fin.at[q], fin_ss.at[q])
    wait(wmeta.at[:, own, :], meta_ss)

    def drain(t, carry):
        wait(stat_s.at[t], stat_ss.at[t])
        wait(smain.at[t, 0 : (nx * ny - 1) * MAIN, :], main_ss.at[t])
        wait(srest.at[t, 0 : (ny - 1) * yblk, :], yrest_ss.at[t])
        wait(xrest.at[t, 0 : (nx - 1) * xblk, :], xrest_ss.at[t])
        for i in range(n_chunk):
            n = size(i)
            quarter = act.at[t, i, 0 : n // 4, :]
            wait(core_in.at[t, i, 0 : n // 2, :], core_ss.at[t, i])
            wait(ysend.at[t, i, 0 : n // 4, :], y_ss.at[t, i])
            wait(quarter, acty_ss.at[t, i])
            wait(quarter, actc_ss.at[t, i])
            wait(quarter, actf_ss.at[t, i])
        wait(smain.at[t, 0 : (nx * ny - 1) * MAIN, :], back_ss.at[t])
        wait(back_x.at[t, 0 : (nx - 1) * xblk, :], backx_ss.at[t])
        wait(back_y.at[t, 0 : (ny - 1) * yblk, :], backy_ss.at[t])
        return carry

    lax.fori_loop(0, TICKS, drain, 0)


def body(section_inputs, incoming, norm_gain, in_weights, down_weights, expert_ids, route_weights):
    ns, count = lax.axis_size("section"), lax.axis_size("expert")
    nx = NX
    ny = count // (2 * nx)
    half = ny // 2
    experts = nx * half
    tok = section_inputs.shape[1]
    ds, ff = in_weights.shape[1], down_weights.shape[2]
    order = sorted(range(half), key=lambda d: (-min(d, half - d), d))
    n_chunk = half + 1
    rest_at, fwd_slot = 2, 1
    dims = (ns, nx, ny, tok, ds, ff, order, rest_at, fwd_slot)
    both = 2 * tok
    n_main, n_rest = experts * MAIN, experts * REST
    n_rows = n_main + n_rest
    most = max(2 * nx * MAIN, nx * ny * REST)
    rest_rows = nx * ny * REST

    def vmem(*shape, dtype=BF16):
        return pltpu.VMEM(shape, dtype)

    def dma(*shape):
        return pltpu.SemaphoreType.DMA(shape) if shape else pltpu.SemaphoreType.DMA

    n = n_chunk
    scratch = [
        vmem(ds, 2 * ff), vmem(ds, ff), vmem(2, 2, both, ds), vmem(2, both, 128, dtype=F32),
        vmem(2, n_rows, both), vmem(2, both, n_rows),
        vmem(2, both, 128, dtype=F32), vmem(2, both, 128, dtype=F32),
        vmem(2, 2 * n_main, ds), vmem(2, 2 * n_rest, ds), vmem(2, n, most, ds),
        vmem(2, rest_rows, ds), vmem(2, rest_rows, ds),
        vmem(2, n, most, 2 * ff), vmem(2, n, most // 2, 2 * ff), vmem(n, most // 4, 2 * ff, dtype=F32),
        vmem(2, n, most // 4, 2 * ff), vmem(2, n, most // 4, 2 * ff), vmem(2, n, most, ff), vmem(2, n, most, ds),
        vmem(2, rest_rows, ds), vmem(2, rest_rows, ds), vmem(2, 2, n_rows, ds),
        vmem(2, 2, both, ds), vmem(2, both, ds), vmem(2, tok, ds),
        dma(2), dma(2, 2), dma(2, 2), dma(), dma(), dma(2), dma(2), dma(2), dma(2, n),
        dma(2), dma(2), dma(2), dma(2, n), dma(2, n), dma(2, n), dma(2, n), dma(2, n), dma(2, n),
        dma(2, n), dma(2, n), dma(2, n), dma(2), dma(2), dma(2), dma(2), dma(2),
        dma(2), dma(2), dma(2), dma(2),
    ]
    in_vmem = pl.BlockSpec(memory_space=pltpu.VMEM)
    anywhere = pl.BlockSpec(memory_space=pl.ANY)
    slots = 2 * 2 * n_rows
    return pl.pallas_call(
        functools.partial(kernel, dims),
        out_shape=jax.ShapeDtypeStruct(section_inputs.shape, section_inputs.dtype),
        in_specs=[in_vmem, in_vmem, in_vmem, anywhere, anywhere, in_vmem, in_vmem],
        out_specs=in_vmem,
        scratch_shapes=scratch,
        compiler_params=pltpu.CompilerParams(
            collective_id=0, has_side_effects=True, vmem_limit_bytes=48 * 1024 * 1024
        ),
        cost_estimate=pl.CostEstimate(
            flops=2 * slots * ds * 3 * ff, bytes_accessed=2 * ds * 3 * ff, transcendentals=slots * ff
        ),
        name="relay",
    )(section_inputs, incoming, norm_gain, in_weights, down_weights, expert_ids, route_weights)


def solution(mesh):
    placed = (
        P("section", "expert", None),
        P(None, "expert", None),
        P("section", None),
        P("section", "expert", None),
        P("section", "expert", None),
        P(None, "section", "expert", None),
        P(None, "section", "expert", None),
    )
    return jax.shard_map(
        body, mesh=mesh, in_specs=placed, out_specs=P("section", "expert", None), check_vma=False
    )
```

time: 305 us -> 178 us (0.58)
  Pallas kernels: 0 us -> 170 us
  waiting for transfers between devices: 152 us -> 0 us
  starting transfers between devices: 53 us -> 0 us
  blocking collectives: 39.5 us -> 0 us
  local copies, waits for them, and re-layouts: 27.4 us -> 7.67 us
  matrix products: 16.1 us -> 0 us
  other arithmetic: 14.7 us -> 0 us
    pallas_call x0 -> x1, Pallas kernels: none -> 170 us  [body(): pl.pallas_call(functools.partial(kernel, dims), out_shape=jax.ShapeDtypeS...]
    all_to_all x3 -> x0, waiting for transfers between devices: 101 us -> none  [the longest x2 66.7 us: body(): lax.all_to_all(produced, 'expert', split_axis=0, concat_axis=0, tiled=True)]
    ppermute x9 -> x0, waiting for transfers between devices: 51.6 us -> none  [the longest x8 44.4 us: swapped(): return lax.ppermute(block, axis, route)]
    all_to_all x1 -> x0, blocking collectives: 39.5 us -> none  [body(): lax.all_to_all(outgoing, 'expert', split_axis=0, concat_axis=0, tiled=True)]
    all_to_all x3 -> x0, starting transfers between devices: 30.3 us -> none  [the longest x1 18.2 us: body(): lax.all_to_all(outgoing, 'expert', split_axis=0, concat_axis=0, tiled=True)]
    ppermute x9 -> x0, starting transfers between devices: 22.7 us -> none  [the longest x8 21.4 us: swapped(): return lax.ppermute(block, axis, route)]
    dot_general x8 -> x0, matrix products: 16.1 us -> none  [the longest x2 9.42 us: body(): jnp.dot(token_rows, in_weights[0], preferred_element_type=jnp.float32)]
    convert_element_type x5 -> x0, local copies, waits for them, and re-layouts: 12.3 us -> none  [the longest x2 10.9 us: body(): partial_value.reshape(row_total, 2, hidden_units).astype(jnp.float32)]
  transfers between devices with their start and end apart: 12 -> 0, of which waited for: 12 -> 0; matrix products, arithmetic and copies ran while one was open for 1% -> 0% of each run, Pallas kernels for 0% -> 0%
where the time goes in v1:
time: 178 us
  Pallas kernels  170 us (96%)
  local copies, waits for them, and re-layouts  7.67 us (4%)
    pallas_call x1, Pallas kernels, body(): pl.pallas_call(functools.partial(kernel, dims), out_shape=jax.ShapeDtypeS...  170 us
    unnamed x13, local copies, waits for them, and re-layouts  7.67 us

profile of v1, /device:TPU:1, one launch (start us, length us, event | category | flops | bytes accessed | tf_op | source)
XLA Modules:
  0.0 177.9 jit_solution(12035318053250851415)
XLA Ops:
  0.0 0.8 copy.8.ids_ref
  0.8 0.8 copy.9.rw_ref
  1.6 0.0 copy-start
  1.6 1.5 copy-done
  3.1 0.0 copy-start.1
  3.1 1.2 copy-done.1
  4.3 0.0 copy-start.2
  4.3 1.0 copy-done.2
  5.3 0.0 copy-start.3
  5.3 1.0 copy-done.3
  6.3 0.0 copy-start.4
  6.3 0.7 copy-done.4
  7.0 170.2 %relay.1 = bf16[1,64,2560]{2,1,0:T(8,128)(2,1)S(1)} custom-call(bf16[1,64,2560]{2,1,0:T(8,128)(2,1)S(1)} %copy-done.2, bf16[1,64,2560]{2,1,0:T(8,128)(2,1)S(1)} %copy-done.3, f32[1,2560]{1,0:T(1,128)S(1)} %copy-done.4, bf16[1,640,1536]{2,1,0:T(8,128)(2,1)S(1)} %copy-done, bf16[1,640,768]{2,1,0:T(8,128)(2,1)S(1)} %copy-done.1, ...), custom_call_target="tpu_custom_call" | custom-call | flops 3774873600 | bytes 2949120 | tf_op jit(solution)/shard_map/relay/pallas_call | solution.py:428
  177.1 0.7 copy.11
Async XLA Ops:
  1.6 1.6 copy-start
  3.1 1.2 copy-start.1
  4.3 1.0 copy-start.2
  5.3 1.0 copy-start.3
  6.3 0.7 copy-start.4

commit v2 on v1

v2 whole, which is shorter than its diff:
```python
import functools

import jax
import jax.numpy as jnp
from jax import lax
from jax.experimental import pallas as pl
from jax.experimental.pallas import tpu as pltpu
from jax.sharding import PartitionSpec as P

TICKS = 2
CAP = 10
NX = 4
MAIN = 16
REST = 4
BF16 = jnp.bfloat16
F32 = jnp.float32


def dot(a, b):
    return jnp.dot(a, b, preferred_element_type=F32)


def iota(shape, dim):
    return lax.broadcasted_iota(jnp.int32, shape, dim)


def kernel(
    dims,
    x_hbm, inc_hbm, gain_hbm, win_hbm, wdn_hbm, ids_ref, rw_ref,
    out_ref,
    state, inc, gain, win, wdn, wmeta, pm, bm, normed, smain, srest, recv, yrest, xrest,
    part, y_in, act, prod, back_x, back_y, ret, mix_s, mix_r, new, hand,
    load, w_ss, w_rs, meta_ss, meta_rs, norm_ss, norm_rs, main_ss, chunk_rs,
    yrest_ss, yrest_rs, xrest_ss, y_ss, y_rs, acty_ss, acty_rs,
    back_ss, backx_ss, backx_rs, backy_ss, back_rs, mix_ss, mix_rs, hand_ss, hand_rs,
):
    ns, nx, ny, tok, ds, ff, groups, chunks, fwd_slot = dims
    half = ny // 2
    nm, nh = nx // 2, half // 2
    both = 2 * tok
    wide = 2 * ds
    n_main = nm * half * MAIN
    yblk = nx * REST
    xblk = half * REST
    n_rest = nh * yblk
    n_rows = n_main + n_rest
    group_rows = 2 * nm * MAIN
    rest_rows = nx * xblk
    width = 4 * ds

    s = lax.axis_index("section")
    me = lax.axis_index("expert")
    x = me // (2 * ny)
    y = (me // 2) % ny
    c = me % 2
    p = y % 2
    k = y // 2
    parities = (p, 1 - p)

    def at(dx, to_y):
        return {"section": s, "expert": (((x + dx + nx) % nx) * ny + to_y) * 2 + c}

    sibling = {"section": s, "expert": me + 1 - 2 * c}
    partner = {"section": s, "expert": (x * ny + y + 1 - 2 * p) * 2 + c}
    ahead = {"section": (s + 1) % ns, "expert": me}
    behind = {"section": (s + ns - 1) % ns, "expert": me}

    def send(src, dst, ss, rs, device):
        pltpu.make_async_remote_copy(
            src_ref=src, dst_ref=dst, send_sem=ss, recv_sem=rs, device_id=device,
            device_id_type=pl.DeviceIdType.MESH,
        ).start()

    def copy(src, dst, sem):
        pltpu.make_async_copy(src, dst, sem).start()

    def wait(ref, sem):
        pltpu.make_async_copy(ref, ref, sem).wait()

    def rows(start, count):
        return pl.ds(pl.multiple_of(start, count & -count), count)

    own = rows(c * tok, tok)
    other = rows((1 - c) * tok, tok)
    slice_own = rows(c * ds, ds)
    slice_other = rows((1 - c) * ds, ds)

    copy(x_hbm.at[0], state.at[0], load.at[0])
    copy(gain_hbm, gain, load.at[1])
    copy(win_hbm.at[0], win.at[slice_own, :], load.at[2])
    copy(wdn_hbm.at[0], wdn.at[slice_own, :], load.at[3])
    copy(inc_hbm.at[0], inc, load.at[4])

    barrier = pltpu.get_barrier_semaphore()
    peers = [at(dx, (y + dy) % ny) for dy in range(ny) for dx in range(nx) if (dx, dy) != (0, 0)]
    peers += [sibling, ahead, behind]
    for device in peers:
        pl.semaphore_signal(barrier, inc=1, device_id=device, device_id_type=pl.DeviceIdType.MESH)

    lane = iota((128, tok), 0)
    for t in range(TICKS):
        ids = ids_ref[t, 0]
        rw = rw_ref[t, 0]
        w = jnp.where(ids[0:1] == lane, rw[0:1], 0.0) + jnp.where(ids[1:2] == lane, rw[1:2], 0.0)
        if tok < 128:
            w = jnp.concatenate([w, jnp.zeros((128, 128 - tok), F32)], axis=1)
        wmeta[t, own, :] = jnp.transpose(w)[:tok]

    def normalise(t):
        v = state[t].astype(F32)
        scale = lax.rsqrt(jnp.sum(v * v, axis=-1, keepdims=True) * (1.0 / width) + 1e-6)
        normed[t, own, :] = (v * scale * gain[...]).astype(BF16)

    wait(state.at[0], load.at[0])
    wait(gain, load.at[1])
    normalise(0)
    pl.semaphore_wait(barrier, len(peers))
    send(wmeta.at[:, own, :], wmeta.at[:, own, :], meta_ss, meta_rs, sibling)

    def earlier(shape, rank_dim):
        a, b = iota(shape, rank_dim), iota(shape, 1 - rank_dim)
        return ((b < a) & (b // tok == a // tok)).astype(BF16)

    def slot_of(j):
        m = j // (half * MAIN)
        main_expert = ((x - c - 2 * m + 2 * nx) % nx) * half + (j // MAIN) % half
        i = j - n_main
        rest_expert = ((i % yblk) // REST) * half + (k - c - 2 * (i // yblk) + 2 * half) % half
        is_main = j < n_main
        return jnp.where(is_main, main_expert, rest_expert), jnp.where(is_main, j % MAIN, MAIN + i % REST)

    def pick_table(t):
        w = jnp.transpose(wmeta[t])
        member = (w > 0).astype(BF16)
        number = dot(member, earlier((both, both), 1)) + (CAP * (iota((128, both), 1) // tok)).astype(F32)
        to_expert, _ = slot_of(iota((n_rows, 128), 0))
        spread = (to_expert == iota((n_rows, 128), 1)).astype(BF16)
        _, to_number = slot_of(iota((n_rows, both), 0))
        hit = (dot(spread, member) > 0.5) & (dot(spread, number.astype(BF16)) == to_number.astype(F32))
        pm[t] = hit.astype(F32).astype(BF16)

    def blend_table(t):
        w = wmeta[t]
        member = (w > 0).astype(BF16)
        number = dot(earlier((both, both), 0), member) + (CAP * (iota((both, 128), 0) // tok)).astype(F32)
        to_expert, _ = slot_of(iota((128, n_rows), 1))
        spread = (to_expert == iota((128, n_rows), 0)).astype(BF16)
        _, to_number = slot_of(iota((both, n_rows), 1))
        hit = (dot(member, spread) > 0.5) & (dot(number.astype(BF16), spread) == to_number.astype(F32))
        bm[t] = jnp.where(hit, dot(w.astype(BF16), spread), 0.0).astype(BF16)

    def shuffle(out_dim):
        o = iota((rest_rows, rest_rows), out_dim)
        r = iota((rest_rows, rest_rows), 1 - out_dim)
        dx, source, j = o // xblk, (o % xblk) // REST, o % REST
        return (r == source * yblk + ((x - dx + nx) % nx) * REST + j).astype(F32).astype(BF16)

    start, chunk_of, first, size, row = {}, {}, [], [], 0
    for i, count in enumerate(chunks):
        first.append(row)
        for g in groups[len(start) : len(start) + count]:
            start[g], chunk_of[g] = row, i
            row += rest_rows if g is None else group_rows
        size.append(row - first[i])
    members = [[g for g in groups if chunk_of[g] == i] for i in range(len(chunks))]

    def blocks(i):
        return [(g, flip, m) for m in range(nm)[::-1] for flip in range(2) for g in members[i] if g is not None]

    def self_or_send(is_self, src, dst, ss, rs, device):
        if not is_self:
            send(src, dst, ss, rs, device)
            return

        @pl.when(c == 0)
        def _():
            copy(src, dst, rs)

        @pl.when(c == 1)
        def _():
            send(src, dst, ss, rs, device)

    def tick(t, carry):
        send(normed.at[t, own, :], normed.at[t, own, :], norm_ss.at[t], norm_rs.at[t], sibling)

        @pl.when(t == 0)
        def _():
            wait(win.at[slice_own, :], load.at[2])
            send(win.at[slice_own, :], win.at[slice_own, :], w_ss.at[0], w_rs.at[0], sibling)
            wait(wdn.at[slice_own, :], load.at[3])
            send(wdn.at[slice_own, :], wdn.at[slice_own, :], w_ss.at[1], w_rs.at[1], sibling)
            wait(wmeta.at[:, other, :], meta_rs)
            pick_table(0)

        wait(normed.at[t, other, :], norm_rs.at[t])
        for q in range(2):
            all_rows = normed[t, :, q * wide : (q + 1) * wide]
            srest[t, q] = dot(pm[t, n_main:, :], all_rows).astype(BF16)
        for h in range(nh):
            to_k = (k - c - 2 * h + 2 * half) % half
            for flip, to_p in enumerate(parities):
                self_or_send(
                    h == 0 and flip == 0,
                    srest.at[t, to_p, h * yblk : (h + 1) * yblk, :], yrest.at[t, rows((2 * h + p) * yblk, yblk), :],
                    yrest_ss.at[t], yrest_rs.at[t], at(0, 2 * to_k + to_p),
                )
        for q in range(2):
            all_rows = normed[t, :, q * wide : (q + 1) * wide]
            smain[t, q] = dot(pm[t, :n_main, :], all_rows).astype(BF16)
        for i in range(len(chunks)):
            for pairs, flip, m in blocks(i):
                to_k, to_p = (k - pairs + half) % half, parities[flip]
                self_or_send(
                    pairs == 0 and flip == 0 and m == 0,
                    smain.at[t, to_p, rows((m * half + to_k) * MAIN, MAIN), :],
                    recv.at[t, rows(start[pairs] + (p * nm + m) * MAIN, MAIN), :],
                    main_ss.at[t], chunk_rs.at[t, i], at(-c - 2 * m + nx, 2 * to_k + to_p),
                )

        @pl.when(t == 0)
        def _():
            blend_table(0)
            pick_table(1)
            blend_table(1)
            wait(inc, load.at[4])
            wait(win.at[slice_other, :], w_rs.at[0])
            wait(wdn.at[slice_other, :], w_rs.at[1])

        def forward_rest():
            wait(yrest.at[t], yrest_rs.at[t])
            xrest[t] = dot(shuffle(0), yrest[t]).astype(BF16)
            for dx in range(nx)[::-1]:
                src = xrest.at[t, dx * xblk : (dx + 1) * xblk, :]
                dst = recv.at[t, start[None] + dx * xblk : start[None] + (dx + 1) * xblk, :]
                if dx == 0:
                    copy(src, dst, chunk_rs.at[t, chunk_of[None]])
                else:
                    send(src, dst, xrest_ss.at[t], chunk_rs.at[t, chunk_of[None]], at(-dx, y))

        def stage_a(i):
            a, n = first[i], size[i]
            wait(recv.at[t, a : a + n, :], chunk_rs.at[t, i])
            lhs = recv[t, a : a + n, :]
            tile = ff // 2 if (ff // 2) % 128 == 0 else ff
            for j in range(0, 2 * ff, tile):
                part[t, a : a + n, j : j + tile] = dot(lhs, win[:, j : j + tile]).astype(BF16)
            send(
                part.at[t, rows(a + (1 - p) * (n // 2), n // 2), :], y_in.at[t, a // 2 : (a + n) // 2, :],
                y_ss.at[t, i], y_rs.at[t, i], partner,
            )

        def stage_c(i):
            a, n = first[i], size[i]
            wait(y_in.at[t, a // 2 : (a + n) // 2, :], y_rs.at[t, i])
            mine = rows(a + p * (n // 2), n // 2)
            pre = part[t, mine, :].astype(F32) + y_in[t, a // 2 : (a + n) // 2, :].astype(F32)
            gate, up = pre[:, :ff], pre[:, ff:]
            act[t, mine, :] = (gate / (1.0 + jnp.exp(-gate)) * up).astype(BF16)
            send(act.at[t, mine, :], act.at[t, mine, :], acty_ss.at[t, i], acty_rs.at[t, i], partner)

        def stage_e(i):
            a, n = first[i], size[i]
            wait(act.at[t, rows(a + (1 - p) * (n // 2), n // 2), :], acty_rs.at[t, i])
            prod[t, a : a + n, :] = lax.dot_general(
                act[t, a : a + n, :], wdn[...], (((1,), (1,)), ((), ())), preferred_element_type=F32
            ).astype(BF16)
            if chunk_of[None] == i:
                for dx in range(nx)[::-1]:
                    src = prod.at[t, start[None] + dx * xblk : start[None] + (dx + 1) * xblk, :]
                    dst = back_x.at[t, dx * xblk : (dx + 1) * xblk, :]
                    if dx == 0:
                        copy(src, dst, backx_rs.at[t])
                    else:
                        send(src, dst, backx_ss.at[t], backx_rs.at[t], at(dx, y))
            for pairs, flip, m in blocks(i):
                to_k, to_p = (k + pairs) % half, parities[flip]
                self_or_send(
                    pairs == 0 and flip == 0 and m == 0,
                    prod.at[t, rows(start[pairs] + (to_p * nm + m) * MAIN, MAIN), :],
                    ret.at[t, p, rows((m * half + k) * MAIN, MAIN), :],
                    back_ss.at[t], back_rs.at[t], at(c + 2 * m, 2 * to_k + to_p),
                )

        def return_rest():
            wait(back_x.at[t], backx_rs.at[t])
            back_y[t] = dot(shuffle(1), back_x[t]).astype(BF16)
            for h in range(nh):
                to_k = (k + c + 2 * h) % half
                for flip, to_p in enumerate(parities):
                    self_or_send(
                        h == 0 and flip == 0,
                        back_y.at[t, rows((2 * h + to_p) * yblk, yblk), :],
                        ret.at[t, p, n_main + h * yblk : n_main + (h + 1) * yblk, :],
                        backy_ss.at[t], back_rs.at[t], at(0, 2 * to_k + to_p),
                    )

        n_chunk = len(chunks)
        for n in range(n_chunk + 3):
            if n == fwd_slot:
                forward_rest()
            if n == chunk_of[None] + 3:
                return_rest()
            if 0 <= n - 2 < n_chunk:
                stage_e(n - 2)
            if 0 <= n - 1 < n_chunk:
                stage_c(n - 1)
            if n < n_chunk:
                stage_a(n)

        wait(ret.at[t], back_rs.at[t])
        for q in range(2):
            mix_s[t, q] = dot(bm[t, other, :], ret[t, q]).astype(BF16)
            send(mix_s.at[t, q], mix_r.at[t, q], mix_ss.at[t, q], mix_rs.at[t, q], sibling)
        for q in range(2):
            mixed = state[t, :, q * wide : (q + 1) * wide].astype(F32) + dot(bm[t, own, :], ret[t, q])
            wait(mix_r.at[t, q], mix_rs.at[t, q])
            new[t, q] = (mixed + mix_r[t, q].astype(F32)).astype(BF16)

            @pl.when(t == 0)
            def _():
                send(new.at[0, q], hand.at[q], hand_ss.at[q], hand_rs.at[q], ahead)

        @pl.when(t == 0)
        def _():
            for q in range(2):
                wait(hand.at[q], hand_rs.at[q])
                part_of = slice(q * wide, (q + 1) * wide)
                state[1, :, part_of] = jnp.where(s == 0, inc[:, part_of], hand[q])
            normalise(1)

        return carry

    lax.fori_loop(0, TICKS, tick, 0)
    for q in range(2):
        out_ref[0, :, q * wide : (q + 1) * wide] = new[1, q]

    for q in range(2):
        wait(hand.at[q], hand_ss.at[q])
    wait(wmeta.at[:, own, :], meta_ss)
    wait(win.at[slice_own, :], w_ss.at[0])
    wait(wdn.at[slice_own, :], w_ss.at[1])

    def drain(t, carry):
        def sent(ref, block, count, sem):
            @pl.when(c == 0)
            def _():
                wait(ref.at[t, 0 : block * count, :], sem.at[t])

            @pl.when(c == 1)
            def _():
                wait(ref.at[t, 0 : block * (count + 1), :], sem.at[t])

        wait(normed.at[t, own, :], norm_ss.at[t])
        sent(recv, MAIN, 2 * nm * half - 1, main_ss)
        sent(yrest, yblk, 2 * nh - 1, yrest_ss)
        wait(xrest.at[t, 0 : (nx - 1) * xblk, :], xrest_ss.at[t])
        for i in range(len(chunks)):
            a, n = first[i], size[i]
            wait(y_in.at[t, a // 2 : (a + n) // 2, :], y_ss.at[t, i])
            wait(act.at[t, a // 2 : (a + n) // 2, :], acty_ss.at[t, i])
        sent(recv, MAIN, 2 * nm * half - 1, back_ss)
        wait(back_x.at[t, 0 : (nx - 1) * xblk, :], backx_ss.at[t])
        sent(yrest, yblk, 2 * nh - 1, backy_ss)
        for q in range(2):
            wait(mix_s.at[t, q], mix_ss.at[t, q])
        return carry

    lax.fori_loop(0, TICKS, drain, 0)


def body(section_inputs, incoming, norm_gain, in_weights, down_weights, expert_ids, route_weights):
    ns, count = lax.axis_size("section"), lax.axis_size("expert")
    nx = NX
    ny = count // (2 * nx)
    half = ny // 2
    tok = section_inputs.shape[1]
    ds, ff = in_weights.shape[1], down_weights.shape[2]
    groups = [None] + sorted(range(half), key=lambda d: (-min(d, half - d), d))
    chunks = [2, 3] if half == 4 else [2, 1]
    fwd_slot = 0
    dims = (ns, nx, ny, tok, ds, ff, groups, chunks, fwd_slot)
    both, wide = 2 * tok, 2 * ds
    nm, nh = nx // 2, half // 2
    n_main, n_rest = nm * half * MAIN, nh * nx * REST
    n_rows = n_main + n_rest
    rest_rows = nx * half * REST
    work = half * 2 * nm * MAIN + rest_rows

    def vmem(*shape, dtype=BF16):
        return pltpu.VMEM(shape, dtype)

    def dma(*shape):
        return pltpu.SemaphoreType.DMA(shape) if shape else pltpu.SemaphoreType.DMA

    n = len(chunks)
    scratch = [
        vmem(2, tok, 2 * wide), vmem(tok, 2 * wide), vmem(1, 2 * wide, dtype=F32),
        vmem(wide, 2 * ff), vmem(wide, ff), vmem(2, both, 128, dtype=F32),
        vmem(2, n_rows, both), vmem(2, both, n_rows), vmem(2, both, 2 * wide),
        vmem(2, 2, n_main, wide), vmem(2, 2, n_rest, wide), vmem(2, work, wide),
        vmem(2, rest_rows, wide), vmem(2, rest_rows, wide),
        vmem(2, work, 2 * ff), vmem(2, work // 2, 2 * ff), vmem(2, work, ff), vmem(2, work, wide),
        vmem(2, rest_rows, wide), vmem(2, rest_rows, wide), vmem(2, 2, n_rows, wide),
        vmem(2, 2, tok, wide), vmem(2, 2, tok, wide), vmem(2, 2, tok, wide), vmem(2, tok, wide),
        dma(5), dma(2), dma(2), dma(), dma(), dma(2), dma(2), dma(2), dma(2, n),
        dma(2), dma(2), dma(2), dma(2, n), dma(2, n), dma(2, n), dma(2, n),
        dma(2), dma(2), dma(2), dma(2), dma(2), dma(2, 2), dma(2, 2), dma(2), dma(2),
    ]
    in_vmem = pl.BlockSpec(memory_space=pltpu.VMEM)
    anywhere = pl.BlockSpec(memory_space=pl.ANY)
    return pl.pallas_call(
        functools.partial(kernel, dims),
        out_shape=jax.ShapeDtypeStruct(section_inputs.shape, section_inputs.dtype),
        in_specs=[anywhere] * 5 + [in_vmem] * 2,
        out_specs=in_vmem,
        scratch_shapes=scratch,
        compiler_params=pltpu.CompilerParams(
            collective_id=0, has_side_effects=True, vmem_limit_bytes=60 * 1024 * 1024
        ),
        cost_estimate=pl.CostEstimate(
            flops=2 * 2 * work * wide * 3 * ff, bytes_accessed=2 * ds * 3 * ff, transcendentals=work * ff
        ),
        name="relay",
    )(
        section_inputs, incoming, norm_gain, in_weights, down_weights,
        jnp.swapaxes(expert_ids, 2, 3), jnp.swapaxes(route_weights, 2, 3),
    )


def solution(mesh):
    placed = (
        P("section", "expert", None),
        P(None, "expert", None),
        P("section", None),
        P("section", "expert", None),
        P("section", "expert", None),
        P(None, "section", "expert", None),
        P(None, "section", "expert", None),
    )
    return jax.shard_map(
        body, mesh=mesh, in_specs=placed, out_specs=P("section", "expert", None), check_vma=False
    )
```

time: 178 us -> 157 us (0.88)
  Pallas kernels: 170 us -> 155 us
  local copies, waits for them, and re-layouts: 7.67 us -> 1.72 us
    pallas_call x1, Pallas kernels: 170 us -> 155 us  [body(): pl.pallas_call(functools.partial(kernel, dims), out_shape=jax.ShapeDtypeS...]
    unnamed x13 -> x1, local copies, waits for them, and re-layouts: 7.67 us -> 1.72 us
where the time goes in v2:
time: 157 us
  Pallas kernels  155 us (99%)
  local copies, waits for them, and re-layouts  1.72 us (1%)
    pallas_call x1, Pallas kernels, body(): pl.pallas_call(functools.partial(kernel, dims), out_shape=jax.ShapeDtypeS...  155 us

profile of v2, /device:TPU:1, one launch (start us, length us, event | category | flops | bytes accessed | tf_op | source)
XLA Modules:
  0.0 156.6 jit_solution(16696335546981860773)
XLA Ops:
  0.0 154.9 %relay.1 = bf16[1,64,2560]{2,1,0:T(8,128)(2,1)} custom-call(bf16[1,64,2560]{2,1,0:T(8,128)(2,1)} %x_hbm.1, bf16[1,64,2560]{2,1,0:T(8,128)(2,1)} %inc_hbm.1, f32[1,2560]{1,0:T(1,128)} %gain_hbm.1, bf16[1,640,1536]{2,1,0:T(8,128)(2,1)} %win_hbm.1, bf16[1,640,768]{2,1,0:T(8,128)(2,1)} %wdn_hbm.1, s32[2,1,2,64]{3,2,1,0:T(2,128)} %bitcast.2, f32[2,1,2,64]{3,2,1,0:T(2,128)} %bitcast.3), custom_call_target="tpu_custom_call" | custom-call | flops 3774873600 | bytes 2949120 | tf_op jit(solution)/shard_map/relay/pallas_call | solution.py:411
  154.9 1.7 %copy.9 = bf16[1,64,2560]{2,1,0:T(8,128)(2,1)} copy(bf16[1,64,2560]{2,1,0:T(8,128)(2,1)} %relay.1) | data formatting | bytes 655360

commit v3 on v2

--- a/solution.py
+++ b/solution.py
@@ -34,7 +34,7 @@
     yrest_ss, yrest_rs, xrest_ss, y_ss, y_rs, acty_ss, acty_rs,
     back_ss, backx_ss, backx_rs, backy_ss, back_rs, mix_ss, mix_rs, hand_ss, hand_rs,
 ):
-    ns, nx, ny, tok, ds, ff, groups, chunks, fwd_slot = dims
+    ns, nx, ny, tok, ds, ff, groups, chunks, fwd_slot, cuts, piece = dims
     half = ny // 2
     nm, nh = nx // 2, half // 2
     both = 2 * tok
@@ -44,6 +44,7 @@
     xblk = half * REST
     n_rest = nh * yblk
     n_rows = n_main + n_rest
+    parts = list(enumerate(slice(a, b) for a, b in zip([0] + cuts, cuts)))
     group_rows = 2 * nm * MAIN
     rest_rows = nx * xblk
     width = 4 * ds
@@ -166,6 +167,10 @@
 
     def blocks(i):
         return [(g, flip, m) for m in range(nm)[::-1] for flip in range(2) for g in members[i] if g is not None]
+
+    def pieces(i):
+        b = min(piece, size[i] // 2)
+        return [(v // b, v, b) for v in range(0, size[i] // 2, b)]
 
     def self_or_send(is_self, src, dst, ss, rs, device):
         if not is_self:
@@ -244,55 +249,60 @@
             tile = ff // 2 if (ff // 2) % 128 == 0 else ff
             for j in range(0, 2 * ff, tile):
                 part[t, a : a + n, j : j + tile] = dot(lhs, win[:, j : j + tile]).astype(BF16)
-            send(
-                part.at[t, rows(a + (1 - p) * (n // 2), n // 2), :], y_in.at[t, a // 2 : (a + n) // 2, :],
-                y_ss.at[t, i], y_rs.at[t, i], partner,
-            )
+            for u, v, b in pieces(i):
+                send(
+                    part.at[t, rows(a + (1 - p) * (n // 2) + v, b), :], y_in.at[t, a // 2 + v : a // 2 + v + b, :],
+                    y_ss.at[t, i], y_rs.at[t, i, u], partner,
+                )
 
         def stage_c(i):
             a, n = first[i], size[i]
-            wait(y_in.at[t, a // 2 : (a + n) // 2, :], y_rs.at[t, i])
-            mine = rows(a + p * (n // 2), n // 2)
-            pre = part[t, mine, :].astype(F32) + y_in[t, a // 2 : (a + n) // 2, :].astype(F32)
-            gate, up = pre[:, :ff], pre[:, ff:]
-            act[t, mine, :] = (gate / (1.0 + jnp.exp(-gate)) * up).astype(BF16)
-            send(act.at[t, mine, :], act.at[t, mine, :], acty_ss.at[t, i], acty_rs.at[t, i], partner)
+            for u, v, b in pieces(i):
+                wait(y_in.at[t, a // 2 + v : a // 2 + v + b, :], y_rs.at[t, i, u])
+                mine = rows(a + p * (n // 2) + v, b)
+                pre = part[t, mine, :].astype(F32) + y_in[t, a // 2 + v : a // 2 + v + b, :].astype(F32)
+                gate, up = pre[:, :ff], pre[:, ff:]
+                act[t, mine, :] = (gate / (1.0 + jnp.exp(-gate)) * up).astype(BF16)
+                send(act.at[t, mine, :], act.at[t, mine, :], acty_ss.at[t, i], acty_rs.at[t, i], partner)
 
         def stage_e(i):
             a, n = first[i], size[i]
             wait(act.at[t, rows(a + (1 - p) * (n // 2), n // 2), :], acty_rs.at[t, i])
-            prod[t, a : a + n, :] = lax.dot_general(
-                act[t, a : a + n, :], wdn[...], (((1,), (1,)), ((), ())), preferred_element_type=F32
-            ).astype(BF16)
-            if chunk_of[None] == i:
-                for dx in range(nx)[::-1]:
-                    src = prod.at[t, start[None] + dx * xblk : start[None] + (dx + 1) * xblk, :]
-                    dst = back_x.at[t, dx * xblk : (dx + 1) * xblk, :]
-                    if dx == 0:
-                        copy(src, dst, backx_rs.at[t])
-                    else:
-                        send(src, dst, backx_ss.at[t], backx_rs.at[t], at(dx, y))
-            for pairs, flip, m in blocks(i):
-                to_k, to_p = (k + pairs) % half, parities[flip]
-                self_or_send(
-                    pairs == 0 and flip == 0 and m == 0,
-                    prod.at[t, rows(start[pairs] + (to_p * nm + m) * MAIN, MAIN), :],
-                    ret.at[t, p, rows((m * half + k) * MAIN, MAIN), :],
-                    back_ss.at[t], back_rs.at[t], at(c + 2 * m, 2 * to_k + to_p),
-                )
+            lhs = act[t, a : a + n, :]
+            for h, cols in parts:
+                prod[t, a : a + n, cols] = lax.dot_general(
+                    lhs, wdn[cols, :], (((1,), (1,)), ((), ())), preferred_element_type=F32
+                ).astype(BF16)
+                if chunk_of[None] == i:
+                    for dx in range(nx)[::-1]:
+                        src = prod.at[t, start[None] + dx * xblk : start[None] + (dx + 1) * xblk, cols]
+                        dst = back_x.at[t, dx * xblk : (dx + 1) * xblk, cols]
+                        if dx == 0:
+                            copy(src, dst, backx_rs.at[t, h])
+                        else:
+                            send(src, dst, backx_ss.at[t, h], backx_rs.at[t, h], at(dx, y))
+                for pairs, flip, m in blocks(i):
+                    to_k, to_p = (k + pairs) % half, parities[flip]
+                    self_or_send(
+                        pairs == 0 and flip == 0 and m == 0,
+                        prod.at[t, rows(start[pairs] + (to_p * nm + m) * MAIN, MAIN), cols],
+                        ret.at[t, p, rows((m * half + k) * MAIN, MAIN), cols],
+                        back_ss.at[t], back_rs.at[t, h], at(c + 2 * m, 2 * to_k + to_p),
+                    )
 
         def return_rest():
-            wait(back_x.at[t], backx_rs.at[t])
-            back_y[t] = dot(shuffle(1), back_x[t]).astype(BF16)
-            for h in range(nh):
-                to_k = (k + c + 2 * h) % half
-                for flip, to_p in enumerate(parities):
-                    self_or_send(
-                        h == 0 and flip == 0,
-                        back_y.at[t, rows((2 * h + to_p) * yblk, yblk), :],
-                        ret.at[t, p, n_main + h * yblk : n_main + (h + 1) * yblk, :],
-                        backy_ss.at[t], back_rs.at[t], at(0, 2 * to_k + to_p),
-                    )
+            for g, cols in parts:
+                wait(back_x.at[t, :, cols], backx_rs.at[t, g])
+                back_y[t, :, cols] = dot(shuffle(1), back_x[t, :, cols]).astype(BF16)
+                for h in range(nh):
+                    to_k = (k + c + 2 * h) % half
+                    for flip, to_p in enumerate(parities):
+                        self_or_send(
+                            h == 0 and flip == 0,
+                            back_y.at[t, rows((2 * h + to_p) * yblk, yblk), cols],
+                            ret.at[t, p, n_main + h * yblk : n_main + (h + 1) * yblk, cols],
+                            backy_ss.at[t], back_rs.at[t, g], at(0, 2 * to_k + to_p),
+                        )
 
         n_chunk = len(chunks)
         for n in range(n_chunk + 3):
@@ -300,32 +310,38 @@
                 forward_rest()
             if n == chunk_of[None] + 3:
                 return_rest()
+            if 0 <= n - 1 < n_chunk:
+                stage_c(n - 1)
             if 0 <= n - 2 < n_chunk:
                 stage_e(n - 2)
-            if 0 <= n - 1 < n_chunk:
-                stage_c(n - 1)
             if n < n_chunk:
                 stage_a(n)
 
-        wait(ret.at[t], back_rs.at[t])
-        for q in range(2):
-            mix_s[t, q] = dot(bm[t, other, :], ret[t, q]).astype(BF16)
-            send(mix_s.at[t, q], mix_r.at[t, q], mix_ss.at[t, q], mix_rs.at[t, q], sibling)
-        for q in range(2):
-            mixed = state[t, :, q * wide : (q + 1) * wide].astype(F32) + dot(bm[t, own, :], ret[t, q])
-            wait(mix_r.at[t, q], mix_rs.at[t, q])
-            new[t, q] = (mixed + mix_r[t, q].astype(F32)).astype(BF16)
+        for h, cols in parts:
+            wait(ret.at[t, :, :, cols], back_rs.at[t, h])
+            for q in range(2):
+                mix_s[t, q, :, cols] = dot(bm[t, other, :], ret[t, q, :, cols]).astype(BF16)
+            send(mix_s.at[t, :, :, cols], mix_r.at[t, :, :, cols], mix_ss.at[t, h], mix_rs.at[t, h], sibling)
+            mixed = [
+                state[t, :, q * wide + cols.start : q * wide + cols.stop].astype(F32)
+                + dot(bm[t, own, :], ret[t, q, :, cols])
+                for q in range(2)
+            ]
+            wait(mix_r.at[t, :, :, cols], mix_rs.at[t, h])
+            for q in range(2):
+                new[t, q, :, cols] = (mixed[q] + mix_r[t, q, :, cols].astype(F32)).astype(BF16)
 
             @pl.when(t == 0)
             def _():
-                send(new.at[0, q], hand.at[q], hand_ss.at[q], hand_rs.at[q], ahead)
+                send(new.at[0, :, :, cols], hand.at[:, :, cols], hand_ss.at[h], hand_rs.at[h], ahead)
 
         @pl.when(t == 0)
         def _():
-            for q in range(2):
-                wait(hand.at[q], hand_rs.at[q])
-                part_of = slice(q * wide, (q + 1) * wide)
-                state[1, :, part_of] = jnp.where(s == 0, inc[:, part_of], hand[q])
+            for h, cols in parts:
+                wait(hand.at[:, :, cols], hand_rs.at[h])
+                for q in range(2):
+                    part_of = slice(q * wide + cols.start, q * wide + cols.stop)
+                    state[1, :, part_of] = jnp.where(s == 0, inc[:, part_of], hand[q, :, cols])
             normalise(1)
 
         return carry
@@ -334,8 +350,8 @@
     for q in range(2):
         out_ref[0, :, q * wide : (q + 1) * wide] = new[1, q]
 
-    for q in range(2):
-        wait(hand.at[q], hand_ss.at[q])
+    for h, cols in parts:
+        wait(hand.at[:, :, cols], hand_ss.at[h])
     wait(wmeta.at[:, own, :], meta_ss)
     wait(win.at[slice_own, :], w_ss.at[0])
     wait(wdn.at[slice_own, :], w_ss.at[1])
@@ -359,10 +375,10 @@
             wait(y_in.at[t, a // 2 : (a + n) // 2, :], y_ss.at[t, i])
             wait(act.at[t, a // 2 : (a + n) // 2, :], acty_ss.at[t, i])
         sent(recv, MAIN, 2 * nm * half - 1, back_ss)
-        wait(back_x.at[t, 0 : (nx - 1) * xblk, :], backx_ss.at[t])
+        for h, cols in parts:
+            wait(back_x.at[t, 0 : (nx - 1) * xblk, cols], backx_ss.at[t, h])
+            wait(mix_s.at[t, :, :, cols], mix_ss.at[t, h])
         sent(yrest, yblk, 2 * nh - 1, backy_ss)
-        for q in range(2):
-            wait(mix_s.at[t, q], mix_ss.at[t, q])
         return carry
 
     lax.fori_loop(0, TICKS, drain, 0)
@@ -378,7 +394,9 @@
     groups = [None] + sorted(range(half), key=lambda d: (-min(d, half - d), d))
     chunks = [2, 3] if half == 4 else [2, 1]
     fwd_slot = 0
-    dims = (ns, nx, ny, tok, ds, ff, groups, chunks, fwd_slot)
+    cuts = [ds * 4 // 5, ds * 8 // 5, 2 * ds]
+    piece = 32
+    dims = (ns, nx, ny, tok, ds, ff, groups, chunks, fwd_slot, cuts, piece)
     both, wide = 2 * tok, 2 * ds
     nm, nh = nx // 2, half // 2
     n_main, n_rest = nm * half * MAIN, nh * nx * REST
@@ -392,7 +410,7 @@
     def dma(*shape):
         return pltpu.SemaphoreType.DMA(shape) if shape else pltpu.SemaphoreType.DMA
 
-    n = len(chunks)
+    n, h = len(chunks), len(cuts)
     scratch = [
         vmem(2, tok, 2 * wide), vmem(tok, 2 * wide), vmem(1, 2 * wide, dtype=F32),
         vmem(wide, 2 * ff), vmem(wide, ff), vmem(2, both, 128, dtype=F32),
@@ -403,8 +421,8 @@
         vmem(2, rest_rows, wide), vmem(2, rest_rows, wide), vmem(2, 2, n_rows, wide),
         vmem(2, 2, tok, wide), vmem(2, 2, tok, wide), vmem(2, 2, tok, wide), vmem(2, tok, wide),
         dma(5), dma(2), dma(2), dma(), dma(), dma(2), dma(2), dma(2), dma(2, n),
-        dma(2), dma(2), dma(2), dma(2, n), dma(2, n), dma(2, n), dma(2, n),
-        dma(2), dma(2), dma(2), dma(2), dma(2), dma(2, 2), dma(2, 2), dma(2), dma(2),
+        dma(2), dma(2), dma(2), dma(2, n), dma(2, n, work // piece), dma(2, n), dma(2, n),
+        dma(2), dma(2, h), dma(2, h), dma(2), dma(2, h), dma(2, h), dma(2, h), dma(h), dma(h),
     ]
     in_vmem = pl.BlockSpec(memory_space=pltpu.VMEM)
     anywhere = pl.BlockSpec(memory_space=pl.ANY)

time: 157 us -> 151 us (0.962)
  Pallas kernels: 155 us -> 149 us
    pallas_call x1, Pallas kernels: 155 us -> 149 us  [body(): pl.pallas_call(functools.partial(kernel, dims), out_shape=jax.ShapeDtypeS...]
where the time goes in v3:
time: 151 us
  Pallas kernels  149 us (99%)
  local copies, waits for them, and re-layouts  1.72 us (1%)
    pallas_call x1, Pallas kernels, body(): pl.pallas_call(functools.partial(kernel, dims), out_shape=jax.ShapeDtypeS...  149 us

profile of v3, /device:TPU:1, one launch (start us, length us, event | category | flops | bytes accessed | tf_op | source)
XLA Modules:
  0.0 151.1 jit_solution(15643627111397875776)
XLA Ops:
  0.0 149.4 %relay.1 = bf16[1,64,2560]{2,1,0:T(8,128)(2,1)} custom-call(bf16[1,64,2560]{2,1,0:T(8,128)(2,1)} %x_hbm.1, bf16[1,64,2560]{2,1,0:T(8,128)(2,1)} %inc_hbm.1, f32[1,2560]{1,0:T(1,128)} %gain_hbm.1, bf16[1,640,1536]{2,1,0:T(8,128)(2,1)} %win_hbm.1, bf16[1,640,768]{2,1,0:T(8,128)(2,1)} %wdn_hbm.1, s32[2,1,2,64]{3,2,1,0:T(2,128)} %bitcast.2, f32[2,1,2,64]{3,2,1,0:T(2,128)} %bitcast.3), custom_call_target="tpu_custom_call" | custom-call | flops 3774873600 | bytes 2949120 | tf_op jit(solution)/shard_map/relay/pallas_call | solution.py:429
  149.4 1.7 %copy.9 = bf16[1,64,2560]{2,1,0:T(8,128)(2,1)} copy(bf16[1,64,2560]{2,1,0:T(8,128)(2,1)} %relay.1) | data formatting | bytes 655360

commit v4 on v3

--- a/solution.py
+++ b/solution.py
@@ -265,22 +265,35 @@
                 act[t, mine, :] = (gate / (1.0 + jnp.exp(-gate)) * up).astype(BF16)
                 send(act.at[t, mine, :], act.at[t, mine, :], acty_ss.at[t, i], acty_rs.at[t, i], partner)
 
+        def down(a, n, cols):
+            prod[t, a : a + n, cols] = lax.dot_general(
+                act[t, a : a + n, :], wdn[cols, :], (((1,), (1,)), ((), ())), preferred_element_type=F32
+            ).astype(BF16)
+
+        def arrived(i):
+            a, n = first[i], size[i]
+            wait(act.at[t, rows(a + (1 - p) * (n // 2), n // 2), :], acty_rs.at[t, i])
+
+        def send_rest():
+            arrived(chunk_of[None])
+            for h, cols in parts:
+                down(start[None], rest_rows, cols)
+                for dx in range(nx)[::-1]:
+                    src = prod.at[t, start[None] + dx * xblk : start[None] + (dx + 1) * xblk, cols]
+                    dst = back_x.at[t, dx * xblk : (dx + 1) * xblk, cols]
+                    if dx == 0:
+                        copy(src, dst, backx_rs.at[t, h])
+                    else:
+                        send(src, dst, backx_ss.at[t, h], backx_rs.at[t, h], at(dx, y))
+
         def stage_e(i):
             a, n = first[i], size[i]
-            wait(act.at[t, rows(a + (1 - p) * (n // 2), n // 2), :], acty_rs.at[t, i])
-            lhs = act[t, a : a + n, :]
+            if chunk_of[None] == i:
+                a, n = a + rest_rows, n - rest_rows
+            else:
+                arrived(i)
             for h, cols in parts:
-                prod[t, a : a + n, cols] = lax.dot_general(
-                    lhs, wdn[cols, :], (((1,), (1,)), ((), ())), preferred_element_type=F32
-                ).astype(BF16)
-                if chunk_of[None] == i:
-                    for dx in range(nx)[::-1]:
-                        src = prod.at[t, start[None] + dx * xblk : start[None] + (dx + 1) * xblk, cols]
-                        dst = back_x.at[t, dx * xblk : (dx + 1) * xblk, cols]
-                        if dx == 0:
-                            copy(src, dst, backx_rs.at[t, h])
-                        else:
-                            send(src, dst, backx_ss.at[t, h], backx_rs.at[t, h], at(dx, y))
+                down(a, n, cols)
                 for pairs, flip, m in blocks(i):
                     to_k, to_p = (k + pairs) % half, parities[flip]
                     self_or_send(
@@ -308,10 +321,12 @@
         for n in range(n_chunk + 3):
             if n == fwd_slot:
                 forward_rest()
-            if n == chunk_of[None] + 3:
-                return_rest()
+            if n == chunk_of[None] + 2:
+                send_rest()
             if 0 <= n - 1 < n_chunk:
                 stage_c(n - 1)
+            if n == chunk_of[None] + 2:
+                return_rest()
             if 0 <= n - 2 < n_chunk:
                 stage_e(n - 2)
             if n < n_chunk:

time: 151 us -> 151 us (level)
  no operation moved by 1% of the time
where the time goes in v4:
time: 151 us
  Pallas kernels  149 us (99%)
  local copies, waits for them, and re-layouts  1.72 us (1%)
    pallas_call x1, Pallas kernels, body(): pl.pallas_call(functools.partial(kernel, dims), out_shape=jax.ShapeDtypeS...  149 us

profile of v4, /device:TPU:1, one launch (start us, length us, event | category | flops | bytes accessed | tf_op | source)
XLA Modules:
  0.0 151.1 jit_solution(12035968523429077772)
XLA Ops:
  0.0 149.4 %relay.1 = bf16[1,64,2560]{2,1,0:T(8,128)(2,1)} custom-call(bf16[1,64,2560]{2,1,0:T(8,128)(2,1)} %x_hbm.1, bf16[1,64,2560]{2,1,0:T(8,128)(2,1)} %inc_hbm.1, f32[1,2560]{1,0:T(1,128)} %gain_hbm.1, bf16[1,640,1536]{2,1,0:T(8,128)(2,1)} %win_hbm.1, bf16[1,640,768]{2,1,0:T(8,128)(2,1)} %wdn_hbm.1, s32[2,1,2,64]{3,2,1,0:T(2,128)} %bitcast.2, f32[2,1,2,64]{3,2,1,0:T(2,128)} %bitcast.3), custom_call_target="tpu_custom_call" | custom-call | flops 3774873600 | bytes 2949120 | tf_op jit(solution)/shard_map/relay/pallas_call | solution.py:444
  149.4 1.7 %copy.9 = bf16[1,64,2560]{2,1,0:T(8,128)(2,1)} copy(bf16[1,64,2560]{2,1,0:T(8,128)(2,1)} %relay.1) | data formatting | bytes 655360
